TPU v7x, 32 devices: a whole 2x2x4 slice. The times are simulated.
32 devices in a mesh: dp: 16 (over z, y, core), seq: 2 (over x).
Axes of the slice: x: 2, y: 2, z: 4, core: 2. Of those that a mesh axis runs over, the one named last changes fastest.
Arguments:
- tile_feats: bfloat16 [8192, 2048], P('dp'), may hold values from -6 to 6
- tile_pos: int32 [16, 512], P('dp'), may hold values from -1 to 511, as said below
- slide_count: int32 [16], P('dp'), may hold values from 128 to 512, as said below
- w_proj: bfloat16 [2048, 768], P(None, 'seq'), may hold values from -0.125 to 0.125
- emb_grad: bfloat16 [16, 512, 768], P('dp', 'seq'), may hold values from -6 to 6
- ln_gain: float32 [768], replicated, may hold values from 0.25 to 1.75
- w_qkv: bfloat16 [768, 2304], P('dp'), may hold values from -1.5 to 1.5
- w_out: bfloat16 [768, 768], P('dp'), may hold values from -0.21875 to 0.21875
Outputs:
- slide_emb: bfloat16 [16, 512, 768], P('dp', 'seq')
- attn_branch: bfloat16 [16, 512, 768], P('dp', 'seq')
- proj_grad: float32 [2048, 768], P(None, 'seq')
Inputs may be any that keep to these rules, and one draw needn't show every extreme that they name: `tile_pos`: slot j of a row belongs to slide j // 32. Each position below a slide's slide_count is held by exactly one slot of that slide over all rows; all other slots hold -1. `slide_count`: some slide is full.
All inputs are finite; a program needn't handle non-finite values.
Results may differ from a plain program's by a relative error of at most 0.017.
The roundings to bfloat16 on the way count: a program that leaves them out, or rounds other values in their place, can miss the bound.
Values may be sent and summed in bfloat16 or wider, within the bound.
A program may use at most 128 MiB of HBM per device.

v0:
```python
import jax
import jax.numpy as jnp
from jax import lax
from jax.sharding import PartitionSpec as P

D = 768
HEAD_COUNT = 12
HEAD_WIDTH = 64
DILATION_STEP = 4
NEGATIVE = -1e30
EPSILON = 1e-05


def selection_shift(values, heads, dilation):
    length = values.shape[1]
    rest = values.shape[2:]
    shaped = values.reshape((heads, length // dilation, dilation) + rest)
    return jnp.stack(
        [shaped[head_number, :, head_number % dilation] for head_number in range(heads)]
    )


def insertion_shift(values, chosen, heads, dilation):
    length = values.shape[1]
    rest = values.shape[2:]
    shaped = values.reshape((heads, length // dilation, dilation) + rest)
    shift_amounts = jnp.arange(heads, dtype=jnp.int32) % dilation
    select = jnp.arange(dilation, dtype=jnp.int32)[None, :] == shift_amounts[:, None]
    select = select.reshape((heads, 1, dilation) + (1,) * len(rest))
    merged = jnp.where(select, chosen[:, :, None], shaped)
    return merged.reshape(values.shape)


def local(tile_feats, tile_pos, slide_count, w_proj, emb_grad, ln_gain, w_qkv, w_out):
    seq_count = lax.axis_size("seq")
    seq_index = lax.axis_index("seq")
    slot_rows = tile_feats.shape[0]
    nearby_length = emb_grad.shape[1]
    slide_len = nearby_length * seq_count
    inner = HEAD_COUNT * HEAD_WIDTH
    scale = HEAD_WIDTH ** (-0.5)
    tile_count = slide_count[0]
    emb_part = jnp.dot(tile_feats, w_proj, preferred_element_type=jnp.float32).astype(jnp.bfloat16)
    feature_part = emb_part.shape[1]
    positions = tile_pos.reshape(slot_rows)
    arrived, arrived_pos = (
        lax.all_to_all(emb_part, "dp", split_axis=0, concat_axis=0, tiled=True),
        lax.all_to_all(positions, "dp", split_axis=0, concat_axis=0, tiled=True),
    )
    target = jnp.where(arrived_pos >= 0, arrived_pos, slide_len).astype(jnp.int32)
    slide_rows = (
        jnp.zeros((slide_len + 1, feature_part), jnp.bfloat16).at[target].set(arrived)[:slide_len]
    )
    local_emb = lax.all_to_all(slide_rows, "seq", split_axis=0, concat_axis=1, tiled=True)
    widened = local_emb.astype(jnp.float32)
    center = jnp.mean(widened, axis=-1, keepdims=True)
    spread = jnp.mean(jnp.square(widened - center), axis=-1, keepdims=True)
    normed = ((widened - center) * lax.rsqrt(spread + EPSILON) * ln_gain).astype(jnp.bfloat16)
    columns = normed
    projected = jnp.dot(
        columns, lax.all_gather(w_qkv, "dp", axis=0, tiled=True), preferred_element_type=jnp.float32
    )
    projected = projected.astype(jnp.bfloat16)
    query_rows = projected[:, :inner].reshape(nearby_length, HEAD_COUNT, HEAD_WIDTH)
    key_matrix = projected[:, inner : 2 * inner].reshape(nearby_length, HEAD_COUNT, HEAD_WIDTH)
    value_matrix = projected[:, 2 * inner :].reshape(nearby_length, HEAD_COUNT, HEAD_WIDTH)
    sequence_position = seq_index * nearby_length + jnp.arange(nearby_length, dtype=jnp.int32)
    occupied = sequence_position < tile_count
    shift_amounts = jnp.arange(HEAD_COUNT, dtype=jnp.int32) % DILATION_STEP
    local_scores = (
        jnp.einsum("qhd,khd->hqk", query_rows, key_matrix, preferred_element_type=jnp.float32)
        * scale
    )
    local_ok = jnp.broadcast_to(occupied[None, None, :], local_scores.shape)
    nearby_maximum = jnp.max(jnp.where(local_ok, local_scores, NEGATIVE), axis=-1)
    local_weight = jnp.where(local_ok, jnp.exp(local_scores - nearby_maximum[..., None]), 0.0)
    nearby_sum = jnp.sum(local_weight, axis=-1)
    nearby_accumulator = jnp.einsum("hqk,khd->hqd", local_weight, value_matrix.astype(jnp.float32))
    stepped_queries = query_rows.reshape(
        nearby_length // DILATION_STEP, DILATION_STEP, HEAD_COUNT, HEAD_WIDTH
    )
    selected_query = jnp.stack(
        [
            stepped_queries[:, head_number % DILATION_STEP, head_number, :]
            for head_number in range(HEAD_COUNT)
        ]
    )
    key_value = jnp.concatenate([key_matrix, value_matrix], axis=-1)
    flat_rows = key_value.reshape(nearby_length, HEAD_COUNT * 2 * HEAD_WIDTH)
    portion = lax.all_gather(flat_rows, "seq", axis=0, tiled=True)
    row_counts = portion.shape[0]
    head_split = (row_counts + DILATION_STEP - 1) // DILATION_STEP
    shaped = portion.reshape(row_counts, HEAD_COUNT, 2 * HEAD_WIDTH)
    leading_index = shift_amounts % DILATION_STEP
    index_of_row = (
        leading_index[:, None] + DILATION_STEP * jnp.arange(head_split, dtype=jnp.int32)[None, :]
    )
    inside = index_of_row < row_counts
    safe_index = jnp.minimum(index_of_row, row_counts - 1)
    head_index = jnp.arange(HEAD_COUNT, dtype=jnp.int32)[:, None]
    chosen = shaped[safe_index, head_index, :]
    key_ok = inside & (index_of_row < tile_count)
    previous_maximum = selection_shift(nearby_maximum, HEAD_COUNT, DILATION_STEP)
    previous_sum = selection_shift(nearby_sum, HEAD_COUNT, DILATION_STEP)
    previous_accumulator = selection_shift(nearby_accumulator, HEAD_COUNT, DILATION_STEP)
    far_scores = (
        jnp.einsum(
            "hqd,hkd->hqk",
            selected_query,
            chosen[..., :HEAD_WIDTH],
            preferred_element_type=jnp.float32,
        )
        * scale
    )
    usable = jnp.broadcast_to(key_ok[:, None, :], far_scores.shape)
    new_max = jnp.maximum(
        previous_maximum, jnp.max(jnp.where(usable, far_scores, NEGATIVE), axis=-1)
    )
    far_weight = jnp.where(usable, jnp.exp(far_scores - new_max[..., None]), 0.0)
    rescale = jnp.exp(previous_maximum - new_max)
    updated_sum = previous_sum * rescale + jnp.sum(far_weight, axis=-1)
    updated_accumulator = previous_accumulator * rescale[..., None] + jnp.einsum(
        "hqk,hkd->hqd", far_weight, chosen[..., HEAD_WIDTH:].astype(jnp.float32)
    )
    complete_sum = insertion_shift(nearby_sum, updated_sum, HEAD_COUNT, DILATION_STEP)
    complete_accumulator = insertion_shift(
        nearby_accumulator, updated_accumulator, HEAD_COUNT, DILATION_STEP
    )
    safe_total = jnp.where(occupied[None, :], complete_sum, 1.0)
    context = jnp.where(occupied[None, :, None], complete_accumulator / safe_total[..., None], 0.0)
    context = context.transpose(1, 0, 2).reshape(nearby_length, inner).astype(jnp.bfloat16)
    columns = context
    branch_out = jnp.dot(
        columns, lax.all_gather(w_out, "dp", axis=0, tiled=True), preferred_element_type=jnp.float32
    )
    attn_branch = branch_out.astype(jnp.bfloat16)
    returned_grad = lax.all_to_all(
        emb_grad.reshape(nearby_length, D), "seq", split_axis=1, concat_axis=0, tiled=True
    )
    padded_grad = jnp.concatenate(
        [returned_grad, jnp.zeros((1, feature_part), jnp.bfloat16)], axis=0
    )
    picked_grad = padded_grad[target]
    slot_grad = lax.all_to_all(picked_grad, "dp", split_axis=0, concat_axis=0, tiled=True)
    grad_part = lax.dot_general(
        tile_feats, slot_grad, (((0,), (0,)), ((), ())), preferred_element_type=jnp.float32
    )
    proj_grad = lax.psum(grad_part, "dp")
    return (local_emb[None], attn_branch[None], proj_grad)


def solution(mesh):
    in_specs = (
        P("dp", None),
        P("dp", None),
        P("dp"),
        P(None, "seq"),
        P("dp", "seq", None),
        P(),
        P("dp", None),
        P("dp", None),
    )
    out_specs = (P("dp", "seq", None), P("dp", "seq", None), P(None, "seq"))
    return jax.shard_map(local, mesh=mesh, in_specs=in_specs, out_specs=out_specs, check_vma=False)
```

profile of v0, /device:TPU:0, one launch (start us, length us, event | category | flops | bytes accessed | tf_op | source)
XLA Modules:
  0.0 267.3 jit_solution(15064173347911541342)
XLA Ops:
  10.5 7.4 %all-to-all-start = ((s32[16,32,1]{1,2,0:T(1,128)}), s32[16,32,1]{1,2,0:T(1,128)S(1)}, u32[]{:S(2)}, u32[]{:S(2)}) async-start(s32[16,32,1]{1,2,0:T(1,128)} %all_to_all.50), calls=%async_computation | async-start | bytes 16384 | tf_op jit(solution)/shard_map/all_to_all | solution.py:48
  17.9 3.5 %convolution_convert_fusion.2 = bf16[512,384]{1,0:T(8,128)(2,1)} fusion(bf16[512,2048]{1,0:T(8,128)(2,1)S(1)} %copy-done, bf16[2048,384]{1,0:T(8,128)(2,1)} %param.11), kind=kOutput, calls=%fused_computation.14 | convolution fusion | flops 805502976 | bytes 4063232 | tf_op jit(solution)/shard_map/dot_general | solution.py:43
  21.3 2.9 %all-to-all-done = s32[16,32,1]{1,2,0:T(1,128)S(1)} async-done(((s32[16,32,1]{1,2,0:T(1,128)}), s32[16,32,1]{1,2,0:T(1,128)S(1)}, u32[]{:S(2)}, u32[]{:S(2)}) %all-to-all-start) | async-done | bytes 2080 | tf_op jit(solution)/shard_map/all_to_all | solution.py:48
  24.2 3.6 %all-to-all-start.1 = ((bf16[16,32,384]{2,1,0:T(8,128)(2,1)}), bf16[16,32,384]{2,1,0:T(8,128)(2,1)S(1)}, u32[]{:S(2)}, u32[]{:S(2)}) async-start(bf16[16,32,384]{2,1,0:T(8,128)(2,1)} %bitcast.1), calls=%async_computation.1 | async-start | bytes 786432 | tf_op jit(solution)/shard_map/all_to_all | solution.py:47
  29.4 12.1 %all-to-all-done.1 = bf16[16,32,384]{2,1,0:T(8,128)(2,1)S(1)} async-done(((bf16[16,32,384]{2,1,0:T(8,128)(2,1)}), bf16[16,32,384]{2,1,0:T(8,128)(2,1)S(1)}, u32[]{:S(2)}, u32[]{:S(2)}) %all-to-all-start.1) | async-done | bytes 393248 | tf_op jit(solution)/shard_map/all_to_all | solution.py:47
  42.2 3.5 %all-to-all-start.3 = ((bf16[256,2,384]{2,0,1:T(8,128)(2,1)}), bf16[256,2,384]{2,0,1:T(8,128)(2,1)S(1)}, u32[]{:S(2)}, u32[]{:S(2)}) async-start(bf16[256,2,384]{2,0,1:T(8,128)(2,1)} %copy.164), calls=%async_computation.3 | async-start | bytes 786432 | tf_op jit(solution)/shard_map/all_to_all | solution.py:137
  45.7 2.9 %scatter_custom_fusion = bf16[513,384]{1,0:T(8,128)(2,1)S(1)} fusion(s32[512]{0:T(512)S(1)} %bitcast.199, bf16[512,384]{1,0:T(8,128)(2,1)} %bitcast.185, bf16[]{:T(256)} %constant.24.clone.1), kind=kCustom, calls=%fused_computation.31 | custom fusion | bytes 394496 | tf_op jit(solution)/shard_map/scatter | solution.py:52
  49.4 3.2 %all-to-all-done.3 = bf16[256,2,384]{2,0,1:T(8,128)(2,1)S(1)} async-done(((bf16[256,2,384]{2,0,1:T(8,128)(2,1)}), bf16[256,2,384]{2,0,1:T(8,128)(2,1)S(1)}, u32[]{:S(2)}, u32[]{:S(2)}) %all-to-all-start.3) | async-done | bytes 393248 | tf_op jit(solution)/shard_map/all_to_all | solution.py:137
  52.6 3.5 %all-to-all-start.2 = ((bf16[2,256,384]{2,1,0:T(8,128)(2,1)}), bf16[2,256,384]{2,1,0:T(8,128)(2,1)S(1)}, u32[]{:S(2)}, u32[]{:S(2)}) async-start(bf16[2,256,384]{2,1,0:T(8,128)(2,1)} %bitcast.3), calls=%async_computation.2 | async-start | bytes 786432 | tf_op jit(solution)/shard_map/all_to_all | solution.py:54
  56.1 2.6 gather_fusion.1
  58.7 3.5 %all-to-all-done.2 = bf16[2,256,384]{2,1,0:T(8,128)(2,1)S(1)} async-done(((bf16[2,256,384]{2,1,0:T(8,128)(2,1)}), bf16[2,256,384]{2,1,0:T(8,128)(2,1)S(1)}, u32[]{:S(2)}, u32[]{:S(2)}) %all-to-all-start.2) | async-done | bytes 393248 | tf_op jit(solution)/shard_map/all_to_all | solution.py:54
  62.1 4.8 %all-to-all-start.4 = ((bf16[16,32,384]{2,1,0:T(8,128)(2,1)}), bf16[16,32,384]{2,1,0:T(8,128)(2,1)}, u32[]{:S(2)}, u32[]{:S(2)}) async-start(bf16[16,32,384]{2,1,0:T(8,128)(2,1)} %bitcast.50), calls=%async_computation.4 | async-start | bytes 786432 | tf_op jit(solution)/shard_map/all_to_all | solution.py:144
  69.3 9.9 %all-to-all-done.4 = bf16[16,32,384]{2,1,0:T(8,128)(2,1)} async-done(((bf16[16,32,384]{2,1,0:T(8,128)(2,1)}), bf16[16,32,384]{2,1,0:T(8,128)(2,1)}, u32[]{:S(2)}, u32[]{:S(2)}) %all-to-all-start.4) | async-done | bytes 393248 | tf_op jit(solution)/shard_map/all_to_all | solution.py:144
  79.2 3.7 %convolution_bitcast_fusion = f32[2048,384]{0,1:T(8,128)} fusion(bf16[512,384]{1,0:T(8,128)(2,1)} %bitcast.51, bf16[512,2048]{1,0:T(8,128)(2,1)S(1)} %copy-done), kind=kOutput, calls=%fused_computation.6 | convolution fusion | flops 805306368 | bytes 5636096 | tf_op jit(solution)/shard_map/dot_general | solution.py:145
  84.4 3.5 %convolution_convert_fusion = bf16[256,2304]{1,0:T(8,128)(2,1)S(1)} fusion(bf16[256,768]{0,1:T(8,128)(2,1)} %fusion.9, bf16[768,2304]{1,0:T(8,128)(2,1)} %all-gather.4.cloned.1.call-done), kind=kOutput, calls=%fused_computation.3 | convolution fusion | flops 906559488 | bytes 5111808 | tf_op jit(solution)/shard_map/dot_general | solution.py:60
  90.8 2.0 pad_maximum_fusion
  95.3 1.9 copy.165
  97.2 87.1 %all-reduce.3.cloned.1.call-done = f32[2048,384]{0,1:T(8,128)} async-done(((f32[2048,384]{0,1:T(8,128)}), f32[2048,384]{0,1:T(8,128)}) %all-reduce.3.cloned.1.call-update) | async-done | bytes 3145744 | tf_op jit(solution)/shard_map/psum | solution.py:148
  184.4 3.5 %copy.166 = f32[2048,384]{1,0:T(8,128)} copy(f32[2048,384]{0,1:T(8,128)} %all-reduce.3.cloned.1.call-done) | data formatting | bytes 6291456
  188.1 1.6 reshape_reshape.3
  189.7 2.4 select_reduce_fusion
  192.1 2.8 %fusion.1 = f32[12,256,64]{1,2,0:T(8,128)S(1)} fusion(bf16[256,12,64]{0,2,1:T(8,128)(2,1)} %bitcast.181, f32[12,256,256]{1,2,0:T(8,128)} %get-tuple-element.69, f32[12,256]{1,0:T(8,128)S(1)} %get-tuple-element.68, pred[256]{0:T(512)(128)(4,1)S(1)} %add_compare_fusion.2), kind=kOutput, calls=%fused_computation.8 | convolution fusion | flops 103022592 | bytes 4337920 | tf_op jit(solution)/shard_map/hqk,khd->hqd/dot_general | solution.py:78
  195.9 1.7 copy.130
  197.6 2.5 fusion.27
  200.7 2.6 fusion.29
  203.3 3.4 %slice_reduce_fusion.12 = (f32[64]{0:T(128)S(1)}, f32[64]{0:T(128)S(1)}, f32[64]{0:T(128)S(1)}, f32[64]{0:T(128)}, f32[64]{0:T(128)}, /*index=5*/f32[64]{0:T(128...) fusion(f32[12,64,4]{0,2,1:T(4,128)S(1)} %bitcast.175), kind=kLoop, calls=%fused_computation.72 | loop fusion | bytes 6144 | tf_op jit(solution)/shard_map/slice | solution.py:19
  206.8 3.4 %slice_reduce_fusion = (f32[64]{0:T(128)}, f32[64]{0:T(128)}, f32[64]{0:T(128)}, f32[64]{0:T(128)}, f32[64]{0:T(128)}, /*index=5*/f32[64]{0:T(128)}, f32[64]{0:T...) fusion(f32[12,64,4]{0,2,1:T(4,128)S(1)} %bitcast.176), kind=kLoop, calls=%fused_computation.60 | loop fusion | bytes 6144 | tf_op jit(solution)/shard_map/slice | solution.py:19
  229.7 2.6 copy.156
  232.3 17.9 %gather_fusion = bf16[1536,128]{1,0:T(8,128)(2,1)S(1)} fusion(bf16[512,12,128]{2,0,1:T(8,128)(2,1)} %copy.156, s32[1536]{0:T(1024)S(1)} %fusion.21), kind=kCustom, calls=%fused_computation | custom fusion | bytes 798720 | tf_op jit(solution)/shard_map/gather | solution.py:101
  252.5 1.5 broadcast_in_dim.146
  253.9 2.8 %copy.159 = f32[12,256,64]{1,2,0:T(8,128)} copy(f32[12,256,64]{2,1,0:T(8,128)} %bitcast.168) | data formatting | bytes 1572864 | tf_op jit(solution)/shard_map/jit(_where)/broadcast_in_dim | solution.py:30
  258.3 2.5 fusion.6
  (92 shorter events, 40.4 us)
Async XLA Ops:
  7.2 10.7 %copy-start = (bf16[512,2048]{1,0:T(8,128)(2,1)S(1)}, bf16[512,2048]{1,0:T(8,128)(2,1)}, u32[]{:S(2)}) copy-start(bf16[512,2048]{1,0:T(8,128)(2,1)} %param.8) | copy-start | bytes 6291460
  7.2 77.3 %all-gather.4.cloned.1.call-start = ((), (), s32[]{:S(2)}) async-start(), calls=%async_computation.5 | async-start | bytes 3760128 | tf_op jit(solution)/shard_map/all_gather | solution.py:61
  10.5 13.7 %all-to-all-start = ((s32[16,32,1]{1,2,0:T(1,128)}), s32[16,32,1]{1,2,0:T(1,128)S(1)}, u32[]{:S(2)}, u32[]{:S(2)}) async-start(s32[16,32,1]{1,2,0:T(1,128)} %all_to_all.50), calls=%async_computation | async-start | bytes 16384 | tf_op jit(solution)/shard_map/all_to_all | solution.py:48
  17.9 9.9 %copy-start.2 = (bf16[1,256,768]{2,1,0:T(8,128)(2,1)S(1)}, bf16[1,256,768]{2,1,0:T(8,128)(2,1)}, u32[]{:S(2)}) copy-start(bf16[1,256,768]{2,1,0:T(8,128)(2,1)} %param.12) | copy-start | bytes 1179652
  24.2 17.3 %all-to-all-start.1 = ((bf16[16,32,384]{2,1,0:T(8,128)(2,1)}), bf16[16,32,384]{2,1,0:T(8,128)(2,1)S(1)}, u32[]{:S(2)}, u32[]{:S(2)}) async-start(bf16[16,32,384]{2,1,0:T(8,128)(2,1)} %bitcast.1), calls=%async_computation.1 | async-start | bytes 786432 | tf_op jit(solution)/shard_map/all_to_all | solution.py:47
  41.5 0.7 copy-start.3
  42.2 10.3 %all-to-all-start.3 = ((bf16[256,2,384]{2,0,1:T(8,128)(2,1)}), bf16[256,2,384]{2,0,1:T(8,128)(2,1)S(1)}, u32[]{:S(2)}, u32[]{:S(2)}) async-start(bf16[256,2,384]{2,0,1:T(8,128)(2,1)} %copy.164), calls=%async_computation.3 | async-start | bytes 786432 | tf_op jit(solution)/shard_map/all_to_all | solution.py:137
  52.6 9.6 %all-to-all-start.2 = ((bf16[2,256,384]{2,1,0:T(8,128)(2,1)}), bf16[2,256,384]{2,1,0:T(8,128)(2,1)S(1)}, u32[]{:S(2)}, u32[]{:S(2)}) async-start(bf16[2,256,384]{2,1,0:T(8,128)(2,1)} %bitcast.3), calls=%async_computation.2 | async-start | bytes 786432 | tf_op jit(solution)/shard_map/all_to_all | solution.py:54
  62.1 17.0 %all-to-all-start.4 = ((bf16[16,32,384]{2,1,0:T(8,128)(2,1)}), bf16[16,32,384]{2,1,0:T(8,128)(2,1)}, u32[]{:S(2)}, u32[]{:S(2)}) async-start(bf16[16,32,384]{2,1,0:T(8,128)(2,1)} %bitcast.50), calls=%async_computation.4 | async-start | bytes 786432 | tf_op jit(solution)/shard_map/all_to_all | solution.py:144
  66.9 117.5 %all-reduce.3.cloned.1.call-start = ((), (), s32[]{:S(2)}) async-start(), calls=%async_computation.8 | async-start | bytes 6291456 | tf_op jit(solution)/shard_map/psum | solution.py:148
  82.8 0.7 copy-start.4
  82.9 146.8 %all-gather.6.cloned.1.call-start = ((), (), s32[]{:S(2)}) async-start(), calls=%async_computation.6 | async-start | bytes 2359296 | tf_op jit(solution)/shard_map/all_gather | solution.py:90
  92.8 165.5 %all-gather.8.cloned.1.call-start = ((), (), s32[]{:S(2)}) async-start(), calls=%async_computation.7 | async-start | bytes 1253376 | tf_op jit(solution)/shard_map/all_gather | solution.py:134
  192.1 3.1 %copy-start.1 = (f32[12,256,256]{1,2,0:T(8,128)S(1)}, f32[12,256,256]{1,2,0:T(8,128)}, u32[]{:S(2)}) copy-start(f32[12,256,256]{1,2,0:T(8,128)} %get-tuple-element.69) | copy-start | bytes 9437188
Sparse Core Ops, SparseCore 0:
  10.3 52.3 all-gather.3
  83.0 101.3 all-reduce.2
  185.9 26.3 all-gather.5
  214.4 38.3 all-gather.7
where the time goes:
time: 269 us; the launch traced here: 267 us
  waiting for transfers between devices  120 us (45%)
  local copies, waits for them, and re-layouts  81 us (30%)
  starting transfers between devices  23 us (9%)
  matrix products  20.2 us (8%)
  between operations  14.7 us (5%)
  other arithmetic  8.78 us (3%)
    psum x1, waiting for transfers between devices, local(): proj_grad = lax.psum(grad_part, 'dp')  87.1 us
    unnamed x35, local copies, waits for them, and re-layouts  24 us
    gather x1, local copies, waits for them, and re-layouts, local(): chosen = shaped[safe_index, head_index, :]  17.9 us
    all_to_all x1, waiting for transfers between devices, local(): lax.all_to_all(emb_part, 'dp', split_axis=0, concat_axis=0, tiled=True)  12.1 us
    all_to_all x1, waiting for transfers between devices, local(): lax.all_to_all(picked_grad, 'dp', split_axis=0, concat_axis=0, tiled=True)  9.87 us
    slice x3, local copies, waits for them, and re-layouts, selection_shift(): shaped[head_number, :, head_number % dilation]  9.23 us
    all_to_all x1, starting transfers between devices, local(): lax.all_to_all(positions, 'dp', split_axis=0, concat_axis=0, tiled=True)  7.39 us
  transfers between devices with their start and end apart: 9, of which 6 were waited for; matrix products, arithmetic and copies ran while one was open for 39% of the time, Pallas kernels for 0%

commit v1 on v0

--- a/solution.py
+++ b/solution.py
@@ -9,6 +9,11 @@
 DILATION_STEP = 4
 NEGATIVE = -1e30
 EPSILON = 1e-05
+
+
+def summed_here(x, axis):
+    parts = lax.all_gather(x, axis)
+    return jnp.sum(parts, axis=0)
 
 
 def selection_shift(values, heads, dilation):
@@ -145,7 +150,7 @@
     grad_part = lax.dot_general(
         tile_feats, slot_grad, (((0,), (0,)), ((), ())), preferred_element_type=jnp.float32
     )
-    proj_grad = lax.psum(grad_part, "dp")
+    proj_grad = summed_here(grad_part, "dp")
     return (local_emb[None], attn_branch[None], proj_grad)
 
 

time: 269 us -> 465 us (1.73)
  waiting for transfers between devices: 120 us -> 271 us
  blocking collectives: 0 us -> 25.2 us
  other arithmetic: 8.78 us -> 29.4 us
  local copies, waits for them, and re-layouts: 81 us -> 89.5 us
  starting transfers between devices: 23 us -> 15.4 us
    all_gather x0 -> x1, waiting for transfers between devices: none -> 238 us  [summed_here(): parts = lax.all_gather(x, axis)]
    psum x1 -> x0, waiting for transfers between devices: 87.1 us -> none  [local(): proj_grad = lax.psum(grad_part, 'dp')]
    unnamed x35 -> x38, local copies, waits for them, and re-layouts: 24 us -> 51 us
    all_to_all x0 -> x2, blocking collectives: none -> 25.2 us  [the longest x1 15.9 us: local(): lax.all_to_all(picked_grad, 'dp', split_axis=0, concat_axis=0, tiled=True)]
    reduce_sum x0 -> x1, other arithmetic: none -> 18.3 us  [summed_here(): return jnp.sum(parts, axis=0)]
    all_to_all x2 -> x0, waiting for transfers between devices: 13.3 us -> none  [the longest x1 9.87 us: local(): lax.all_to_all(picked_grad, 'dp', split_axis=0, concat_axis=0, tiled=True)]
    gather x1, local copies, waits for them, and re-layouts: 17.9 us -> 8.29 us  [local(): chosen = shaped[safe_index, head_index, :]]
    all_to_all x1, waiting for transfers between devices: 3.18 us -> 11.9 us  [local(): lax.all_to_all(emb_grad.reshape(nearby_length, D), 'seq', split_axis=1, c...]
  transfers between devices with their start and end apart: 9 -> 7, of which waited for: 6 -> 5; matrix products, arithmetic and copies ran while one was open for 39% -> 13% of each run, Pallas kernels for 0% -> 0%
where the time goes in v1:
time: 465 us; the launch traced here: 464 us
  waiting for transfers between devices  271 us (58%)
  local copies, waits for them, and re-layouts  89.5 us (19%)
  other arithmetic  29.4 us (6%)
  blocking collectives  25.2 us (5%)
  matrix products  17.8 us (4%)
  starting transfers between devices  15.4 us (3%)
  between operations  14.9 us (3%)
    all_gather x1, waiting for transfers between devices, summed_here(): parts = lax.all_gather(x, axis)  238 us
    unnamed x38, local copies, waits for them, and re-layouts  51 us
    reduce_sum x1, other arithmetic, summed_here(): return jnp.sum(parts, axis=0)  18.3 us
    all_to_all x1, blocking collectives, local(): lax.all_to_all(picked_grad, 'dp', split_axis=0, concat_axis=0, tiled=True)  15.9 us
    all_to_all x1, waiting for transfers between devices, local(): lax.all_to_all(emb_part, 'dp', split_axis=0, concat_axis=0, tiled=True)  12.9 us
    all_to_all x1, waiting for transfers between devices, local(): lax.all_to_all(emb_grad.reshape(nearby_length, D), 'seq', split_axis=1, c...  11.9 us
    all_to_all x1, blocking collectives, local(): lax.all_to_all(slide_rows, 'seq', split_axis=0, concat_axis=1, tiled=True)  9.31 us
  transfers between devices with their start and end apart: 7, of which 5 were waited for; matrix products, arithmetic and copies ran while one was open for 13% of the time, Pallas kernels for 0%

profile of v1, /device:TPU:0, one launch (start us, length us, event | category | flops | bytes accessed | tf_op | source)
XLA Modules:
  0.0 463.7 jit_solution(7182529851629736067)
XLA Ops:
  10.5 7.4 %all-to-all-start = ((s32[16,32,1]{1,2,0:T(1,128)}), s32[16,32,1]{1,2,0:T(1,128)S(1)}, u32[]{:S(2)}, u32[]{:S(2)}) async-start(s32[16,32,1]{1,2,0:T(1,128)} %all_to_all.50), calls=%async_computation | async-start | bytes 16384 | tf_op jit(solution)/shard_map/all_to_all | solution.py:53
  17.9 3.4 convolution_convert_fusion.2
  21.3 2.9 all-to-all-done
  24.2 3.7 all-to-all-start.1
  28.7 12.9 %all-to-all-done.1 = bf16[16,32,384]{2,1,0:T(8,128)(2,1)S(1)} async-done(((bf16[16,32,384]{2,1,0:T(8,128)(2,1)}), bf16[16,32,384]{2,1,0:T(8,128)(2,1)S(1)}, u32[]{:S(2)}, u32[]{:S(2)}) %all-to-all-start.1) | async-done | bytes 393248 | tf_op jit(solution)/shard_map/all_to_all | solution.py:52
  41.6 2.4 scatter_custom_fusion
  44.1 9.3 %all_to_all.71 = bf16[2,256,384]{2,1,0:T(8,128)(2,1)S(1)} all-to-all(bf16[2,256,384]{2,1,0:T(8,128)(2,1)S(1)} %bitcast.187), channel_id=1, replica_groups=mesh['dp'=16,'seq'=2] {'seq'}, dimensions={0} | all-to-all | bytes 786432 | tf_op jit(solution)/shard_map/all_to_all | solution.py:59
  54.3 2.3 copy.122
  58.4 4.3 all-gather.6.cloned.1.call-done
  62.7 3.1 convolution_convert_fusion
  68.7 2.1 pad_maximum_fusion
  71.6 1.8 all_to_all.59
  73.4 1.8 copy.161
  75.2 4.2 all-to-all-start.3
  79.4 11.9 %all-to-all-done.3 = bf16[256,2,384]{2,0,1:T(8,128)(2,1)} async-done(((bf16[256,2,384]{2,0,1:T(8,128)(2,1)}), bf16[256,2,384]{2,0,1:T(8,128)(2,1)}, u32[]{:S(2)}, u32[]{:S(2)}) %all-to-all-start.3) | async-done | bytes 393248 | tf_op jit(solution)/shard_map/all_to_all | solution.py:142
  92.4 2.6 gather_fusion.1
  95.0 15.9 %all_to_all.72 = bf16[16,32,384]{2,1,0:T(8,128)(2,1)S(1)} all-to-all(bf16[16,32,384]{2,1,0:T(8,128)(2,1)} %bitcast.186), channel_id=1, replica_groups=mesh['dp'=16,'seq'=2] {'dp'}, dimensions={0} | all-to-all | bytes 786432 | tf_op jit(solution)/shard_map/all_to_all | solution.py:149
  110.9 2.6 convolution_bitcast_fusion
  115.9 1.6 reshape_reshape.3
  117.5 2.4 select_reduce_fusion
  120.0 2.6 fusion
  122.7 2.5 fusion.1
  125.7 2.8 slice_reduce_fusion.12
  128.5 2.8 slice_reduce_fusion
  132.0 2.0 fusion.29
  134.2 1.9 copy.153
  136.1 8.3 %gather_fusion = bf16[1536,128]{1,0:T(8,128)(2,1)S(1)} fusion(bf16[512,12,128]{2,0,1:T(8,128)(2,1)S(1)} %copy.153, s32[1536]{0:T(1024)S(1)} %fusion.21), kind=kCustom, calls=%fused_computation | custom fusion | bytes 798720 | tf_op jit(solution)/shard_map/gather | solution.py:106
  148.8 2.9 fusion.6
  151.6 237.9 %all-gather.12.cloned.1.call-done = f32[32768,384]{0,1:T(8,128)} async-done(((f32[2048,384]{0,1:T(8,128)}), f32[32768,384]{0,1:T(8,128)}) %all-gather.12.cloned.1.call-update) | async-done | bytes 50331664 | tf_op jit(solution)/shard_map/all_gather | solution.py:15
  389.5 45.8 %copy.191 = f32[48,8,16,2048]{3,2,1,0:T(8,128)} copy(f32[48,8,16,2048]{3,1,2,0:T(8,128)} %bitcast.173) | data formatting | bytes 100663296
  435.3 18.3 %bitcast_reduce_fusion = f32[2048,384]{0,1:T(8,128)} fusion(f32[48,8,16,2048]{3,2,1,0:T(8,128)} %copy.191), kind=kLoop, calls=%fused_computation.3 | loop fusion | flops 11796480 | bytes 53477376 | tf_op jit(solution)/shard_map/reduce_sum | solution.py:16
  453.7 3.5 copy.163
  (94 shorter events, 18.9 us)
Async XLA Ops:
  7.2 10.7 %copy-start = (bf16[512,2048]{1,0:T(8,128)(2,1)S(1)}, bf16[512,2048]{1,0:T(8,128)(2,1)}, u32[]{:S(2)}) copy-start(bf16[512,2048]{1,0:T(8,128)(2,1)} %param.8) | copy-start | bytes 6291460
  7.2 55.5 %all-gather.6.cloned.1.call-start = ((), (), s32[]{:S(2)}) async-start(), calls=%async_computation.5 | async-start | bytes 3760128 | tf_op jit(solution)/shard_map/all_gather | solution.py:66
  10.5 13.7 %all-to-all-start = ((s32[16,32,1]{1,2,0:T(1,128)}), s32[16,32,1]{1,2,0:T(1,128)S(1)}, u32[]{:S(2)}, u32[]{:S(2)}) async-start(s32[16,32,1]{1,2,0:T(1,128)} %all_to_all.50), calls=%async_computation | async-start | bytes 16384 | tf_op jit(solution)/shard_map/all_to_all | solution.py:53
  24.2 32.9 %copy-start.5 = (f32[768]{0:T(1024)S(1)}, f32[768]{0:T(1024)}, u32[]{:S(2)}) copy-start(f32[768]{0:T(1024)} %param.13) | copy-start | bytes 9220
  24.2 17.4 %all-to-all-start.1 = ((bf16[16,32,384]{2,1,0:T(8,128)(2,1)}), bf16[16,32,384]{2,1,0:T(8,128)(2,1)S(1)}, u32[]{:S(2)}, u32[]{:S(2)}) async-start(bf16[16,32,384]{2,1,0:T(8,128)(2,1)} %bitcast.1), calls=%async_computation.1 | async-start | bytes 786432 | tf_op jit(solution)/shard_map/all_to_all | solution.py:52
  27.9 106.3 %all-gather.8.cloned.1.call-start = ((), (), s32[]{:S(2)}) async-start(), calls=%async_computation.6 | async-start | bytes 2359296 | tf_op jit(solution)/shard_map/all_gather | solution.py:95
  68.7 22.6 %copy-start.2 = (bf16[256,768]{0,1:T(8,128)(2,1)}, bf16[256,768]{0,1:T(8,128)(2,1)S(1)}, u32[]{:S(2)}) copy-start(bf16[256,768]{0,1:T(8,128)(2,1)S(1)} %copy.124) | copy-start | bytes 1179652
  70.8 77.9 %all-gather.10.cloned.1.call-start = ((), (), s32[]{:S(2)}) async-start(), calls=%async_computation.7 | async-start | bytes 1253376 | tf_op jit(solution)/shard_map/all_gather | solution.py:139
  75.2 16.2 %all-to-all-start.3 = ((bf16[256,2,384]{2,0,1:T(8,128)(2,1)}), bf16[256,2,384]{2,0,1:T(8,128)(2,1)}, u32[]{:S(2)}, u32[]{:S(2)}) async-start(bf16[256,2,384]{2,0,1:T(8,128)(2,1)} %copy.161), calls=%async_computation.3 | async-start | bytes 786432 | tf_op jit(solution)/shard_map/all_to_all | solution.py:142
  79.4 310.2 %all-gather.12.cloned.1.call-start = ((), (), s32[]{:S(2)}) async-start(), calls=%async_computation.8 | async-start | bytes 53477376 | tf_op jit(solution)/shard_map/all_gather | solution.py:15
  113.5 3.9 copy-start.3
  117.5 5.2 %copy-start.4 = (bf16[256,768]{0,1:T(8,128)(2,1)S(1)}, bf16[256,768]{0,1:T(8,128)(2,1)}, u32[]{:S(2)}) copy-start(bf16[256,768]{0,1:T(8,128)(2,1)} %copy.125) | copy-start | bytes 1179652
  435.3 21.9 %copy-start.1 = (bf16[512,2048]{1,0:T(8,128)(2,1)S(1)}, bf16[512,2048]{1,0:T(8,128)(2,1)}, u32[]{:S(2)}) copy-start(bf16[512,2048]{1,0:T(8,128)(2,1)} %param.8) | copy-start | bytes 6291460
Sparse Core Ops, SparseCore 0:
  10.3 52.3 all-gather.5
  70.9 30.3 all-gather.7
  103.7 38.3 all-gather.9
  143.4 246.0 all-gather.11
